TPU v7x, 32 devices: a whole 2x2x4 slice. The times are simulated.
32 devices in a mesh: expert: 32 (over z, y, x, core), hid: 1.
Axes of the slice: x: 2, y: 2, z: 4, core: 2. Of those that a mesh axis runs over, the one named last changes fastest.
Arguments:
- tokens: bfloat16 [4096, 3584], P('expert'), may hold values from -6 to 6
- out_grad: bfloat16 [4096, 3584], P('expert'), may hold values from -4 to 4
- route_ids: int32 [4096, 4], P('expert'), may hold values from 0 to 31, all different within a row; in each aligned block of 128 rows (0 to 127, 128 to 255, ...) at most 24 rows name the same one
- route_gates: float32 [4096, 4], P('expert'), may hold values from 0.1 to 1
- w_gate: bfloat16 [32, 3584, 1024], P('expert', None, 'hid'), may hold values from -0.09375 to 0.09375
- w_up: bfloat16 [32, 3584, 1024], P('expert', None, 'hid'), may hold values from -0.09375 to 0.09375
- w_down: bfloat16 [32, 1024, 3584], P('expert', 'hid'), may hold values from -0.1875 to 0.1875
Outputs:
- token_grad: bfloat16 [4096, 3584], P('expert', 'hid')
- gate_grad: bfloat16 [4096, 4], P('expert')
Inputs may be any that keep to these rules, and one draw needn't show every extreme that they name: `route_ids`: each token names 4 different experts. Among the 128 tokens of one index of expert (aligned blocks of rows), no expert is named more than 24 times, a bound that some block reaches.
All inputs are finite; a program needn't handle non-finite values.
Results may differ from a plain program's by a relative error of at most 0.008.
Values may be sent and summed in bfloat16 or wider, within the bound.
A program may use at most 128 MiB of HBM per device.

v0:
```python
import jax
import jax.numpy as jnp
from jax import lax
from jax.sharding import PartitionSpec as P


def place_rows(source, dest_slot, slot_count):
    return jnp.zeros((slot_count, source.shape[1]), source.dtype).at[dest_slot].set(source)


def body(tokens, out_grad, route_ids, route_gates, w_gate, w_up, w_down):
    expert_count = lax.axis_size("expert")
    pair_count = lax.axis_size("hid")
    tok_rows, model_width = tokens.shape
    top_count = route_ids.shape[1]
    capacity = 3 * tok_rows * top_count // (2 * expert_count)
    slot_count = expert_count * capacity
    half_width = model_width // pair_count
    flat_ids = route_ids.reshape(-1)
    one_hot = (flat_ids[:, None] == jnp.arange(expert_count, dtype=jnp.int32)[None, :]).astype(
        jnp.int32
    )
    earlier = jnp.cumsum(one_hot, axis=0) - one_hot
    slot_index = jnp.sum(earlier * one_hot, axis=1)
    dest_slot = flat_ids * capacity + slot_index
    token_of = jnp.arange(tok_rows * top_count, dtype=jnp.int32) // top_count
    send_x = place_rows(tokens[token_of], dest_slot, slot_count).reshape(
        expert_count, capacity, model_width
    )
    send_d = place_rows(out_grad[token_of], dest_slot, slot_count).reshape(
        expert_count, capacity, model_width
    )
    rows_x, rows_d = (
        lax.all_to_all(send_x, "expert", split_axis=0, concat_axis=0, tiled=True),
        lax.all_to_all(send_d, "expert", split_axis=0, concat_axis=0, tiled=True),
    )
    rows_x = rows_x.reshape(slot_count, model_width)
    rows_d = rows_d.reshape(slot_count, model_width)
    gate_mat = w_gate[0]
    up_mat = w_up[0]
    down_mat = w_down[0]
    contract_last = (((1,), (1,)), ((), ()))
    gate_pre = jnp.dot(rows_x, gate_mat, preferred_element_type=jnp.float32)
    up_pre = jnp.dot(rows_x, up_mat, preferred_element_type=jnp.float32)
    grad_hidden = lax.dot_general(
        rows_d, down_mat, contract_last, preferred_element_type=jnp.float32
    )
    sigma_gate = jax.nn.sigmoid(gate_pre)
    act_gate = gate_pre * sigma_gate
    score_part = jnp.sum(act_gate * up_pre * grad_hidden, axis=1)
    grad_gate_pre = (
        grad_hidden * up_pre * sigma_gate * (1.0 + gate_pre * (1.0 - sigma_gate))
    ).astype(jnp.bfloat16)
    grad_up_pre = (grad_hidden * act_gate).astype(jnp.bfloat16)
    grad_part = lax.dot_general(
        grad_gate_pre, gate_mat, contract_last, preferred_element_type=jnp.float32
    ) + lax.dot_general(grad_up_pre, up_mat, contract_last, preferred_element_type=jnp.float32)
    grad_share = lax.psum_scatter(grad_part, "hid", scatter_dimension=1, tiled=True).astype(
        jnp.bfloat16
    )
    score_full = lax.psum(score_part, "hid").astype(jnp.bfloat16)
    back_grad, back_score = (
        lax.all_to_all(
            grad_share.reshape(expert_count, capacity, half_width),
            "expert",
            split_axis=0,
            concat_axis=0,
            tiled=True,
        ),
        lax.all_to_all(
            score_full.reshape(expert_count, capacity),
            "expert",
            split_axis=0,
            concat_axis=0,
            tiled=True,
        ),
    )
    picked = back_grad.reshape(slot_count, half_width)[dest_slot]
    picked = picked.reshape(tok_rows, top_count, half_width).astype(jnp.float32)
    token_grad = jnp.einsum("tkd,tk->td", picked, route_gates).astype(jnp.bfloat16)
    gate_grad = back_score.reshape(slot_count)[dest_slot].reshape(tok_rows, top_count)
    return (token_grad, gate_grad)


def solution(mesh):
    return jax.shard_map(
        body,
        mesh=mesh,
        in_specs=(
            P("expert", None),
            P("expert", None),
            P("expert", None),
            P("expert", None),
            P("expert", None, "hid"),
            P("expert", None, "hid"),
            P("expert", "hid", None),
        ),
        out_specs=(P("expert", "hid"), P("expert", None)),
        check_vma=False,
    )
```

profile of v0, /device:TPU:0, one launch (start us, length us, event | category | flops | bytes accessed | tf_op | source)
XLA Modules:
  0.0 477.0 jit_solution(12576779367512234791)
XLA Ops:
  0.6 0.0 copy-start
  0.6 0.9 copy.15
  1.5 0.1 eq.29
  1.6 0.1 eq.25
  1.7 0.7 broadcast_multiply_fusion
  2.4 1.2 reduce-window.6
  3.6 0.2 slice_reduce_fusion
  3.9 0.1 copy.14
  4.0 0.1 mul.45
  4.1 0.1 fusion.23
  4.2 0.0 copy-done
  4.2 19.8 %scatter_custom_fusion.1 = bf16[768,3584]{1,0:T(8,128)(2,1)} fusion(s32[512]{0:T(512)S(1)} %bitcast.58, bf16[128,3584]{1,0:T(8,128)(2,1)S(1)} %copy-done, s32[1024]{0:T(1024)S(1)} %pad_clamp_fusion.1, bf16[]{:T(256)} %constant.25.clone.1), kind=kCustom, calls=%fused_computation.17 | custom fusion | bytes 5505026 | tf_op jit(solution)/shard_map/scatter | solution.py:8
  24.1 7.9 %all-to-all-start.1 = ((bf16[32,24,3584]{2,1,0:T(8,128)(2,1)}), bf16[32,24,3584]{2,1,0:T(8,128)(2,1)}, u32[]{:S(2)}, u32[]{:S(2)}) async-start(bf16[32,24,3584]{2,1,0:T(8,128)(2,1)} %bitcast.55), calls=%async_computation.1 | async-start | bytes 11010048 | tf_op jit(solution)/shard_map/all_to_all | solution.py:34
  32.0 18.2 %scatter_custom_fusion = bf16[768,3584]{1,0:T(8,128)(2,1)} fusion(s32[512]{0:T(512)S(1)} %bitcast.59, bf16[128,3584]{1,0:T(8,128)(2,1)} %param.8, s32[1024]{0:T(1024)S(1)} %pad_clamp_fusion.1, bf16[]{:T(256)} %constant.25.clone.1), kind=kCustom, calls=%fused_computation.19 | custom fusion | bytes 5505536 | tf_op jit(solution)/shard_map/scatter | solution.py:8
  50.2 104.3 %all-to-all-done.1 = bf16[32,24,3584]{2,1,0:T(8,128)(2,1)} async-done(((bf16[32,24,3584]{2,1,0:T(8,128)(2,1)}), bf16[32,24,3584]{2,1,0:T(8,128)(2,1)}, u32[]{:S(2)}, u32[]{:S(2)}) %all-to-all-start.1) | async-done | bytes 5505056 | tf_op jit(solution)/shard_map/all_to_all | solution.py:34
  154.5 3.8 all-to-all-start
  158.3 10.9 %fusion.2 = f32[768,1024]{1,0:T(8,128)} fusion(bf16[768,3584]{1,0:T(8,128)(2,1)} %bitcast.8, bf16[1,3584,1024]{2,1,0:T(8,128)(2,1)} %param.11), kind=kOutput, calls=%fused_computation.9 | convolution fusion | flops 5637144576 | bytes 15990784 | tf_op jit(solution)/shard_map/dot_general | solution.py:43
  169.2 10.9 %fusion.6 = f32[768,1024]{1,0:T(8,128)} fusion(bf16[768,3584]{1,0:T(8,128)(2,1)} %bitcast.8, bf16[1,3584,1024]{2,1,0:T(8,128)(2,1)} %param.12), kind=kOutput, calls=%fused_computation.13 | convolution fusion | flops 5637144576 | bytes 15990784 | tf_op jit(solution)/shard_map/dot_general | solution.py:44
  180.1 100.7 %all-to-all-done = bf16[32,24,3584]{2,1,0:T(8,128)(2,1)} async-done(((bf16[32,24,3584]{2,1,0:T(8,128)(2,1)}), bf16[32,24,3584]{2,1,0:T(8,128)(2,1)}, u32[]{:S(2)}, u32[]{:S(2)}) %all-to-all-start) | async-done | bytes 5505056 | tf_op jit(solution)/shard_map/all_to_all | solution.py:35
  280.8 0.0 copy-start.3
  280.8 0.0 copy-start.5
  280.8 11.8 %multiply_reduce_fusion = (bf16[768]{0:T(1024)(128)(2,1)S(1)}, f32[768,1024]{1,0:T(8,128)S(1)}) fusion(f32[768,1024]{1,0:T(8,128)} %fusion.6, f32[768,1024]{1,0:T(8,128)} %fusion.2, bf16[768,3584]{1,0:T(8,128)(2,1)} %bitcast.5, bf16[1,1024,3584]{2,1,0:T(8,128)(2,1)} %param.13), kind=kOutput, calls=%fused_computation.21 | convolution fusion | flops 5642648576 | bytes 22283776 | tf_op jit(solution)/shard_map/dot_general | solution.py:45
  292.6 0.0 copy-start.4
  292.7 0.0 copy-done.3
  292.7 0.0 copy-done.5
  292.7 13.7 %fusion = f32[768,3584]{1,0:T(8,128)} fusion(bf16[1,3584,1024]{2,1,0:T(8,128)(2,1)} %param.11, f32[768,1024]{1,0:T(8,128)S(1)} %copy-done.3, f32[768,1024]{1,0:T(8,128)S(1)} %get-tuple-element.7, f32[768,1024]{1,0:T(8,128)S(1)} %copy-done.5), kind=kOutput, calls=%fused_computation.7 | convolution fusion | flops 5645008896 | bytes 27787264 | tf_op jit(solution)/shard_map/dot_general | solution.py:55
  306.4 0.0 copy-done.4
  306.4 0.7 convert_element_type.42
  307.1 3.3 all-to-all-start.3
  310.4 14.0 %add_convert_fusion = bf16[768,3584]{1,0:T(8,128)(2,1)} fusion(f32[768,3584]{1,0:T(8,128)} %fusion, bf16[1,3584,1024]{2,1,0:T(8,128)(2,1)} %param.12, f32[768,1024]{1,0:T(8,128)} %copy-done.4, f32[768,1024]{1,0:T(8,128)} %fusion.2), kind=kOutput, calls=%fused_computation.6 | convolution fusion | flops 5647368192 | bytes 30146560 | tf_op jit(solution)/shard_map/dot_general | solution.py:57
  324.4 0.0 all-to-all-done.3
  324.4 0.0 copy-start.2
  324.4 6.2 %all-to-all-start.2 = ((bf16[32,24,3584]{2,1,0:T(8,128)(2,1)}), bf16[32,24,3584]{2,1,0:T(8,128)(2,1)}, u32[]{:S(2)}, u32[]{:S(2)}) async-start(bf16[32,24,3584]{2,1,0:T(8,128)(2,1)} %bitcast.56), calls=%async_computation.2 | async-start | bytes 11010048 | tf_op jit(solution)/shard_map/all_to_all | solution.py:63
  330.6 0.0 copy-done.2
  330.6 0.2 copy.20
  330.8 0.1 reduce.1
  330.9 0.1 reshape.144
  331.0 3.5 gather_fusion.1
  334.5 0.1 reshape.145
  334.6 0.7 copy.19
  335.3 117.9 %all-to-all-done.2 = bf16[32,24,3584]{2,1,0:T(8,128)(2,1)} async-done(((bf16[32,24,3584]{2,1,0:T(8,128)(2,1)}), bf16[32,24,3584]{2,1,0:T(8,128)(2,1)}, u32[]{:S(2)}, u32[]{:S(2)}) %all-to-all-start.2) | async-done | bytes 5505056 | tf_op jit(solution)/shard_map/all_to_all | solution.py:63
  453.1 11.2 %gather_fusion = bf16[512,3584]{1,0:T(8,128)(2,1)} fusion(bf16[768,3584]{1,0:T(8,128)(2,1)} %bitcast.12, s32[1024]{0:T(1024)S(1)} %pad_clamp_fusion), kind=kCustom, calls=%fused_computation.2 | custom fusion | bytes 7342080 | tf_op jit(solution)/shard_map/gather | solution.py:78
  464.3 0.0 copy-start.1
  464.3 7.1 %reshape.143 = bf16[128,4,3584]{2,1,0:T(4,128)(2,1)} reshape(bf16[512,3584]{1,0:T(8,128)(2,1)} %gather_fusion) | data formatting | bytes 7340032 | tf_op jit(solution)/shard_map/reshape | solution.py:79
  471.4 4.1 fusion.27
  475.5 1.0 copy.25
  476.5 0.0 copy-done.1
  (7 shorter events, 0.1 us)
Async XLA Ops:
  0.6 3.6 copy-start
  24.1 130.5 %all-to-all-start.1 = ((bf16[32,24,3584]{2,1,0:T(8,128)(2,1)}), bf16[32,24,3584]{2,1,0:T(8,128)(2,1)}, u32[]{:S(2)}, u32[]{:S(2)}) async-start(bf16[32,24,3584]{2,1,0:T(8,128)(2,1)} %bitcast.55), calls=%async_computation.1 | async-start | bytes 11010048 | tf_op jit(solution)/shard_map/all_to_all | solution.py:34
  154.5 126.3 %all-to-all-start = ((bf16[32,24,3584]{2,1,0:T(8,128)(2,1)}), bf16[32,24,3584]{2,1,0:T(8,128)(2,1)}, u32[]{:S(2)}, u32[]{:S(2)}) async-start(bf16[32,24,3584]{2,1,0:T(8,128)(2,1)} %bitcast.54), calls=%async_computation | async-start | bytes 11010048 | tf_op jit(solution)/shard_map/all_to_all | solution.py:35
  280.8 11.8 %copy-start.3 = (f32[768,1024]{1,0:T(8,128)S(1)}, f32[768,1024]{1,0:T(8,128)}, u32[]{:S(2)}) copy-start(f32[768,1024]{1,0:T(8,128)} %fusion.2) | copy-start | bytes 9437188
  280.8 11.8 %copy-start.5 = (f32[768,1024]{1,0:T(8,128)S(1)}, f32[768,1024]{1,0:T(8,128)}, u32[]{:S(2)}) copy-start(f32[768,1024]{1,0:T(8,128)} %fusion.6) | copy-start | bytes 9437188
  292.6 13.7 %copy-start.4 = (f32[768,1024]{1,0:T(8,128)}, f32[768,1024]{1,0:T(8,128)S(1)}, u32[]{:S(2)}) copy-start(f32[768,1024]{1,0:T(8,128)S(1)} %get-tuple-element.7) | copy-start | bytes 9437188
  307.1 17.4 %all-to-all-start.3 = ((bf16[32,1,24]{2,1,0:T(2,128)(2,1)}), bf16[32,1,24]{2,1,0:T(2,128)(2,1)S(1)}, u32[]{:S(2)}, u32[]{:S(2)}) async-start(bf16[32,1,24]{2,1,0:T(2,128)(2,1)} %convert_element_type.42), calls=%async_computation.3 | async-start | bytes 32768 | tf_op jit(solution)/shard_map/all_to_all | solution.py:70
  324.4 6.2 %copy-start.2 = (f32[128,4]{0,1:T(4,128)S(1)}, f32[128,4]{0,1:T(4,128)}, u32[]{:S(2)}) copy-start(f32[128,4]{0,1:T(4,128)} %param.10) | copy-start | bytes 6148
  324.4 128.7 %all-to-all-start.2 = ((bf16[32,24,3584]{2,1,0:T(8,128)(2,1)}), bf16[32,24,3584]{2,1,0:T(8,128)(2,1)}, u32[]{:S(2)}, u32[]{:S(2)}) async-start(bf16[32,24,3584]{2,1,0:T(8,128)(2,1)} %bitcast.56), calls=%async_computation.2 | async-start | bytes 11010048 | tf_op jit(solution)/shard_map/all_to_all | solution.py:63
  464.3 12.2 %copy-start.1 = (bf16[128,3584]{1,0:T(8,128)(2,1)S(1)}, bf16[128,3584]{1,0:T(8,128)(2,1)}, u32[]{:S(2)}) copy-start(bf16[128,3584]{1,0:T(8,128)(2,1)} %param.7) | copy-start | bytes 2752516
where the time goes:
time: 486 us; the launch traced here: 477 us
  waiting for transfers between devices  323 us (66%)
  matrix products  65.3 us (13%)
  local copies, waits for them, and re-layouts  64.1 us (13%)
  starting transfers between devices  21.3 us (4%)
    all_to_all x1, waiting for transfers between devices, body(): lax.all_to_all(grad_share.reshape(expert_count, capacity, half_width), 'e...  118 us
    all_to_all x1, waiting for transfers between devices, body(): lax.all_to_all(send_x, 'expert', split_axis=0, concat_axis=0, tiled=True)  104 us
    all_to_all x1, waiting for transfers between devices, body(): lax.all_to_all(send_d, 'expert', split_axis=0, concat_axis=0, tiled=True)  101 us
    scatter x2, local copies, waits for them, and re-layouts, place_rows(): jnp.zeros((slot_count, source.shape[1]), source.dtype).at[dest_slot]  38 us
    dot_general x1, matrix products, body(): lax.dot_general(grad_up_pre, up_mat, contract_last, preferred_element_typ...  14 us
    dot_general x1, matrix products, body(): lax.dot_general(grad_gate_pre, gate_mat, contract_last, preferred_element...  13.7 us
    dot_general x1, matrix products, body(): lax.dot_general(rows_d, down_mat, contract_last, preferred_element_type=j...  11.8 us
    gather x1, local copies, waits for them, and re-layouts, body(): picked = back_grad.reshape(slot_count, half_width)[dest_slot]  11.2 us
  transfers between devices with their start and end apart: 4, of which 3 were waited for; matrix products, arithmetic and copies ran while one was open for 12% of the time, Pallas kernels for 0%

commit v1 on v0

v1 whole, which is shorter than its diff:
```python
import jax
import jax.numpy as jnp
from jax import lax
from jax.sharding import PartitionSpec as P

BF = jnp.bfloat16
F32 = jnp.float32


def place_rows(source, dest_slot, slot_count):
    return jnp.zeros((slot_count, source.shape[1]), source.dtype).at[dest_slot].set(source)


def flat_body(tokens, out_grad, route_ids, route_gates, w_gate, w_up, w_down):
    expert_count = lax.axis_size("expert")
    pair_count = lax.axis_size("hid")
    tok_rows, model_width = tokens.shape
    top_count = route_ids.shape[1]
    capacity = 3 * tok_rows * top_count // (2 * expert_count)
    slot_count = expert_count * capacity
    half_width = model_width // pair_count
    flat_ids = route_ids.reshape(-1)
    one_hot = (flat_ids[:, None] == jnp.arange(expert_count, dtype=jnp.int32)[None, :]).astype(
        jnp.int32
    )
    earlier = jnp.cumsum(one_hot, axis=0) - one_hot
    slot_index = jnp.sum(earlier * one_hot, axis=1)
    dest_slot = flat_ids * capacity + slot_index
    token_of = jnp.arange(tok_rows * top_count, dtype=jnp.int32) // top_count
    send_x = place_rows(tokens[token_of], dest_slot, slot_count).reshape(
        expert_count, capacity, model_width
    )
    send_d = place_rows(out_grad[token_of], dest_slot, slot_count).reshape(
        expert_count, capacity, model_width
    )
    rows_x, rows_d = (
        lax.all_to_all(send_x, "expert", split_axis=0, concat_axis=0, tiled=True),
        lax.all_to_all(send_d, "expert", split_axis=0, concat_axis=0, tiled=True),
    )
    rows_x = rows_x.reshape(slot_count, model_width)
    rows_d = rows_d.reshape(slot_count, model_width)
    grad_part, score_part = expert_math(rows_x, rows_d, w_gate[0], w_up[0], w_down[0])
    grad_share = lax.psum_scatter(grad_part, "hid", scatter_dimension=1, tiled=True).astype(BF)
    score_full = lax.psum(score_part, "hid").astype(BF)
    back_grad, back_score = (
        lax.all_to_all(
            grad_share.reshape(expert_count, capacity, half_width),
            "expert",
            split_axis=0,
            concat_axis=0,
            tiled=True,
        ),
        lax.all_to_all(
            score_full.reshape(expert_count, capacity),
            "expert",
            split_axis=0,
            concat_axis=0,
            tiled=True,
        ),
    )
    picked = back_grad.reshape(slot_count, half_width)[dest_slot]
    picked = picked.reshape(tok_rows, top_count, half_width).astype(F32)
    token_grad = jnp.einsum("tkd,tk->td", picked, route_gates).astype(BF)
    gate_grad = back_score.reshape(slot_count)[dest_slot].reshape(tok_rows, top_count)
    return (token_grad, gate_grad)


def expert_math(rows_x, rows_d, gate_mat, up_mat, down_mat):
    contract_last = (((1,), (1,)), ((), ()))
    gate_pre = jnp.dot(rows_x, gate_mat, preferred_element_type=F32)
    up_pre = jnp.dot(rows_x, up_mat, preferred_element_type=F32)
    grad_hidden = lax.dot_general(rows_d, down_mat, contract_last, preferred_element_type=F32)
    sigma_gate = jax.nn.sigmoid(gate_pre)
    act_gate = gate_pre * sigma_gate
    score_part = jnp.sum(act_gate * up_pre * grad_hidden, axis=1)
    grad_gate_pre = (
        grad_hidden * up_pre * sigma_gate * (1.0 + gate_pre * (1.0 - sigma_gate))
    ).astype(BF)
    grad_up_pre = (grad_hidden * act_gate).astype(BF)
    grad_part = lax.dot_general(
        grad_gate_pre, gate_mat, contract_last, preferred_element_type=F32
    ) + lax.dot_general(grad_up_pre, up_mat, contract_last, preferred_element_type=F32)
    return grad_part, score_part


def slot_masks(ids, experts, capacity):
    tok_rows = ids.shape[-2]
    hit = ids[..., None] == experts
    named = jnp.any(hit, axis=-2).astype(BF)
    before = jnp.tril(jnp.ones((tok_rows, tok_rows), BF), -1)
    rank = jnp.einsum("ut,...te->...eu", before, named, preferred_element_type=F32)
    named = jnp.swapaxes(named, -1, -2) > 0
    slots = jnp.arange(capacity, dtype=F32)
    place = (rank[..., None, :] == slots[:, None]) & named[..., None, :]
    return hit, place


def plane_body(tokens, out_grad, route_ids, route_gates, w_gate, w_up, w_down):
    n = lax.axis_size("expert")
    plane = 8
    layers = n // plane
    tok_rows, width = tokens.shape
    top_count = route_ids.shape[1]
    capacity = 3 * tok_rows * top_count // (2 * n)
    me = lax.axis_index("expert")
    columns = [[z * plane + q for z in range(layers)] for q in range(plane)]
    planes = [[z * plane + q for q in range(plane)] for z in range(layers)]

    def gather_z(a):
        return lax.all_gather(a, "expert", axis_index_groups=columns)

    def swap(a):
        return lax.all_to_all(
            a, "expert", split_axis=0, concat_axis=0, axis_index_groups=planes, tiled=True
        )

    packed = jnp.concatenate([route_ids.astype(F32), route_gates], axis=1)
    packed = gather_z(packed)
    all_x = gather_z(tokens)
    all_d = gather_z(out_grad)
    ids = packed[..., :top_count].astype(jnp.int32)
    gates = packed[..., top_count:]
    local = (me // plane) * plane + jnp.arange(plane, dtype=jnp.int32)
    hit, place = slot_masks(ids, local, capacity)
    gate_of = jnp.einsum("ztke,ztk->zet", hit.astype(F32), gates, precision="highest")
    place_bf = place.astype(BF)
    weights = jnp.where(place, gate_of[:, :, None, :], 0.0)
    high = weights.astype(BF)
    low = (weights - high.astype(F32)).astype(BF)

    def dispatch(rows):
        send = jnp.einsum("zest,ztd->ezsd", place_bf, rows, preferred_element_type=F32).astype(BF)
        return swap(send.reshape(plane, layers * capacity, width)).reshape(-1, width)

    rows_x = dispatch(all_x)
    rows_d = dispatch(all_d)
    grad_part, score = expert_math(rows_x, rows_d, w_gate[0], w_up[0], w_down[0])
    back = swap(grad_part.astype(BF).reshape(plane, layers * capacity, width))
    back = back.reshape(plane, layers, capacity, width)
    both = jnp.concatenate([high, low], axis=1)
    back2 = jnp.concatenate([back, back], axis=0)
    part = jnp.einsum("zest,ezsd->ztd", both, back2, preferred_element_type=F32)
    token_grad = lax.psum_scatter(
        part.astype(BF), "expert", scatter_dimension=0, axis_index_groups=columns, tiled=False
    )
    scores = lax.all_gather(score.astype(BF), "expert").reshape(n, plane, layers, capacity)
    mine = lax.dynamic_index_in_dim(scores, me % plane, 1, keepdims=False)
    mine = lax.dynamic_index_in_dim(mine, me // plane, 1, keepdims=False)
    hit_own, place_own = slot_masks(route_ids, jnp.arange(n, dtype=jnp.int32), capacity)
    by_expert = jnp.einsum("est,es->te", place_own.astype(F32), mine.astype(F32), precision="highest")
    gate_grad = jnp.sum(jnp.where(hit_own, by_expert[:, None, :], 0.0), axis=2).astype(BF)
    return (token_grad, gate_grad)


def solution(mesh):
    n = mesh.shape["expert"]
    flat = mesh.shape["hid"] != 1 or n % 8 != 0
    return jax.shard_map(
        flat_body if flat else plane_body,
        mesh=mesh,
        in_specs=(
            P("expert", None),
            P("expert", None),
            P("expert", None),
            P("expert", None),
            P("expert", None, "hid"),
            P("expert", None, "hid"),
            P("expert", "hid", None),
        ),
        out_specs=(P("expert", "hid"), P("expert", None)),
        check_vma=False,
    )
```

time: 486 us -> 416 us (0.86); the launches traced: 477 us -> 415 us
  waiting for transfers between devices: 323 us -> 250 us
  local copies, waits for them, and re-layouts: 64.1 us -> 7.04 us
  blocking collectives: 0 us -> 53.9 us
  between operations: 1.24 us -> 13.9 us
  matrix products: 65.3 us -> 73.2 us
  starting transfers between devices: 21.3 us -> 14.3 us
    all_to_all x4 -> x3, waiting for transfers between devices: 323 us -> 104 us  [swap(): lax.all_to_all(a, 'expert', split_axis=0, concat_axis=0, axis_index_group...]
    all_gather x0 -> x2, waiting for transfers between devices: none -> 120 us  [gather_z(): return lax.all_gather(a, 'expert', axis_index_groups=columns)]
    all_gather x0 -> x2, blocking collectives: none -> 53.9 us  [the longest x1 39 us: plane_body(): lax.all_gather(score.astype(BF), 'expert')]
    scatter x2 -> x0, local copies, waits for them, and re-layouts: 38 us -> none  [place_rows(): jnp.zeros((slot_count, source.shape[1]), source.dtype).at[dest_slot]]
    reduce_scatter x0 -> x1, waiting for transfers between devices: none -> 24.3 us  [plane_body(): lax.psum_scatter(part.astype(BF), 'expert', scatter_dimension=0, axis_ind...]
    gather x2 -> x0, local copies, waits for them, and re-layouts: 14.7 us -> none  [the longest x1 11.2 us: body(): picked = back_grad.reshape(slot_count, half_width)[dest_slot]]
    dot_general x6 -> x11, matrix products: 65.3 us -> 73.2 us  [the longest x1 12.7 us: expert_math(): lax.dot_general(grad_gate_pre, gate_mat, contract_last, preferred_element...]
    all_to_all x4 -> x3, starting transfers between devices: 21.3 us -> 14.2 us  [swap(): lax.all_to_all(a, 'expert', split_axis=0, concat_axis=0, axis_index_group...]
  transfers between devices with their start and end apart: 4 -> 6, of which waited for: 3 -> 5; matrix products, arithmetic and copies ran while one was open for 12% -> 9% of each run, Pallas kernels for 0% -> 0%
where the time goes in v1:
time: 416 us; the launch traced here: 415 us
  waiting for transfers between devices  250 us (60%)
  matrix products  73.2 us (18%)
  blocking collectives  53.9 us (13%)
  starting transfers between devices  14.3 us (3%)
  between operations  13.9 us (3%)
  local copies, waits for them, and re-layouts  7.04 us (2%)
    all_gather x2, waiting for transfers between devices, gather_z(): return lax.all_gather(a, 'expert', axis_index_groups=columns)  120 us
    all_to_all x3, waiting for transfers between devices, swap(): lax.all_to_all(a, 'expert', split_axis=0, concat_axis=0, axis_index_group...  104 us
    all_gather x1, blocking collectives, plane_body(): lax.all_gather(score.astype(BF), 'expert')  39 us
    reduce_scatter x1, waiting for transfers between devices, plane_body(): lax.psum_scatter(part.astype(BF), 'expert', scatter_dimension=0, axis_ind...  24.3 us
    all_gather x1, blocking collectives, gather_z(): return lax.all_gather(a, 'expert', axis_index_groups=columns)  14.9 us
    all_to_all x3, starting transfers between devices, swap(): lax.all_to_all(a, 'expert', split_axis=0, concat_axis=0, axis_index_group...  14.2 us
    dot_general x1, matrix products, expert_math(): lax.dot_general(grad_gate_pre, gate_mat, contract_last, preferred_element...  12.7 us
    dot_general x1, matrix products, expert_math(): lax.dot_general(grad_up_pre, up_mat, contract_last, preferred_element_typ...  12.4 us
  transfers between devices with their start and end apart: 6, of which 5 were waited for; matrix products, arithmetic and copies ran while one was open for 9% of the time, Pallas kernels for 0%

profile of v1, /device:TPU:0, one launch (start us, length us, event | category | flops | bytes accessed | tf_op | source)
XLA Modules:
  0.0 415.1 jit_solution(8885934856217605243)
XLA Ops:
  7.2 0.0 all-gather.10.cloned.1.call-start
  7.2 0.7 all-gather.10.cloned.1.call-update
  7.9 0.0 all-gather.8.cloned.1.call-start
  7.9 0.7 all-gather.8.cloned.1.call-update
  8.6 0.7 convert_element_type.69
  9.3 0.7 pad_maximum_fusion.1
  10.0 14.9 %all-gather = f32[512,8]{0,1:T(8,128)S(1)} all-gather(f32[128,8]{0,1:T(8,128)S(1)} %pad_maximum_fusion.1), channel_id=2, replica_groups={{0,8,16,24},{1,9,17,25},{2,10,18,26},{3,11,19,27},{4,12,20,28},{5,13,21..., dimensions={0}, use_global_device_ids=true | all-gather | bytes 20480 | tf_op jit(solution)/shard_map/all_gather | solution.py:110
  24.9 0.1 compare_reduce_fusion
  25.0 0.2 fusion.44
  25.2 59.2 %all-gather.10.cloned.1.call-done = bf16[512,3584]{1,0:T(8,128)(2,1)} async-done(((bf16[128,3584]{1,0:T(8,128)(2,1)}), bf16[512,3584]{1,0:T(8,128)(2,1)}) %all-gather.10.cloned.1.call-update) | async-done | bytes 3670032 | tf_op jit(solution)/shard_map/all_gather | solution.py:110
  84.5 3.6 fusion.17
  88.1 2.9 copy.29
  91.0 4.7 %all-to-all-start.1 = ((bf16[8,96,3584]{2,1,0:T(8,128)(2,1)}), bf16[8,96,3584]{2,1,0:T(8,128)(2,1)}, u32[]{:S(2)}, u32[]{:S(2)}) async-start(bf16[8,96,3584]{2,1,0:T(8,128)(2,1)} %bitcast.66), calls=%async_computation.1 | async-start | bytes 11010048 | tf_op jit(solution)/shard_map/all_to_all | solution.py:113
  95.6 61.1 %all-gather.8.cloned.1.call-done = bf16[512,3584]{1,0:T(8,128)(2,1)} async-done(((bf16[128,3584]{1,0:T(8,128)(2,1)}), bf16[512,3584]{1,0:T(8,128)(2,1)}) %all-gather.8.cloned.1.call-update) | async-done | bytes 3670032 | tf_op jit(solution)/shard_map/all_gather | solution.py:110
  156.7 3.6 fusion.16
  160.4 3.0 copy.28
  163.3 0.0 all-to-all-done.1
  163.3 4.9 %all-to-all-start = ((bf16[8,96,3584]{2,1,0:T(8,128)(2,1)}), bf16[8,96,3584]{2,1,0:T(8,128)(2,1)}, u32[]{:S(2)}, u32[]{:S(2)}) async-start(bf16[8,96,3584]{2,1,0:T(8,128)(2,1)} %bitcast.65), calls=%async_computation | async-start | bytes 11010048 | tf_op jit(solution)/shard_map/all_to_all | solution.py:113
  168.2 10.9 %fusion.4 = f32[768,1024]{1,0:T(8,128)} fusion(bf16[768,3584]{1,0:T(8,128)(2,1)} %bitcast.16, bf16[1,3584,1024]{2,1,0:T(8,128)(2,1)} %param.11), kind=kOutput, calls=%fused_computation.7 | convolution fusion | flops 5637144576 | bytes 15990784 | tf_op jit(solution)/shard_map/dot_general | solution.py:70
  179.0 10.9 %fusion.8 = f32[768,1024]{1,0:T(8,128)} fusion(bf16[768,3584]{1,0:T(8,128)(2,1)} %bitcast.16, bf16[1,3584,1024]{2,1,0:T(8,128)(2,1)} %param.12), kind=kOutput, calls=%fused_computation.11 | convolution fusion | flops 5637144576 | bytes 15990784 | tf_op jit(solution)/shard_map/dot_general | solution.py:71
  189.9 41.2 %all-to-all-done = bf16[8,96,3584]{2,1,0:T(8,128)(2,1)} async-done(((bf16[8,96,3584]{2,1,0:T(8,128)(2,1)}), bf16[8,96,3584]{2,1,0:T(8,128)(2,1)}, u32[]{:S(2)}, u32[]{:S(2)}) %all-to-all-start) | async-done | bytes 5505056 | tf_op jit(solution)/shard_map/all_to_all | solution.py:113
  231.2 0.0 copy-start.1
  231.2 0.0 copy-start.2
  231.2 11.8 %multiply_reduce_fusion = (bf16[768]{0:T(1024)(128)(2,1)S(1)}, f32[768,1024]{1,0:T(8,128)S(1)}) fusion(f32[768,1024]{1,0:T(8,128)} %fusion.8, f32[768,1024]{1,0:T(8,128)} %fusion.4, bf16[768,3584]{1,0:T(8,128)(2,1)} %bitcast.9, bf16[1,1024,3584]{2,1,0:T(8,128)(2,1)} %param.13), kind=kOutput, calls=%fused_computation.19 | convolution fusion | flops 5642648576 | bytes 22283776 | tf_op jit(solution)/shard_map/dot_general | solution.py:72
  243.0 0.0 copy-done.1
  243.0 0.0 copy-done.2
  243.0 12.7 %fusion.2 = f32[768,3584]{1,0:T(8,128)} fusion(bf16[1,3584,1024]{2,1,0:T(8,128)(2,1)} %param.11, f32[768,1024]{1,0:T(8,128)S(1)} %copy-done.1, f32[768,1024]{1,0:T(8,128)S(1)} %get-tuple-element.5, f32[768,1024]{1,0:T(8,128)S(1)} %copy-done.2), kind=kOutput, calls=%fused_computation.5 | convolution fusion | flops 5645008896 | bytes 27787264 | tf_op jit(solution)/shard_map/dot_general | solution.py:80
  255.7 12.4 %add_convert_fusion = bf16[768,3584]{1,0:T(8,128)(2,1)} fusion(f32[768,3584]{1,0:T(8,128)} %fusion.2, bf16[1,3584,1024]{2,1,0:T(8,128)(2,1)} %param.12, f32[768,1024]{1,0:T(8,128)S(1)} %get-tuple-element.5, f32[768,1024]{1,0:T(8,128)S(1)} %copy-done.1), kind=kOutput, calls=%fused_computation.3 | convolution fusion | flops 5647368192 | bytes 30146560 | tf_op jit(solution)/shard_map/dot_general | solution.py:82
  268.1 4.7 %all-to-all-start.2 = ((bf16[8,96,3584]{2,1,0:T(8,128)(2,1)}), bf16[8,96,3584]{2,1,0:T(8,128)(2,1)}, u32[]{:S(2)}, u32[]{:S(2)}) async-start(bf16[8,96,3584]{2,1,0:T(8,128)(2,1)} %bitcast.67), calls=%async_computation.2 | async-start | bytes 11010048 | tf_op jit(solution)/shard_map/all_to_all | solution.py:113
  272.8 0.0 reduce-scatter.2.cloned.1.call-start
  272.8 0.1 fusion.37
  272.9 0.1 select_convert_fusion
  273.0 0.1 fusion.21
  273.1 62.8 %all-to-all-done.2 = bf16[8,96,3584]{2,1,0:T(8,128)(2,1)} async-done(((bf16[8,96,3584]{2,1,0:T(8,128)(2,1)}), bf16[8,96,3584]{2,1,0:T(8,128)(2,1)}, u32[]{:S(2)}, u32[]{:S(2)}) %all-to-all-start.2) | async-done | bytes 5505056 | tf_op jit(solution)/shard_map/all_to_all | solution.py:113
  335.9 6.7 %bitcast_convert_fusion = bf16[4,128,3584]{2,1,0:T(8,128)(2,1)} fusion(bf16[4,8,24,128]{3,2,1,0:T(8,128)(2,1)S(1)} %fusion.21, bf16[4,8,24,128]{3,2,1,0:T(8,128)(2,1)S(1)} %select_convert_fusion, bf16[8,4,24,3584]{3,2,1,0:T(8,128)(2,1)} %bitcast.20), kind=kOutput, calls=%fused_computation.4 | convolution fusion | flops 1416822784 | bytes 9568256 | tf_op jit(solution)/shard_map/zest,ezsd->ztd/dot_general | solution.py:142
  342.7 0.0 copy-start
  342.7 0.0 reduce-scatter.2.cloned.1.call-update
  342.7 0.6 copy-done
  343.4 0.2 fusion.40
  343.6 39.0 %all-gather.4 = bf16[32,1,768]{2,1,0:T(2,128)(2,1)S(1)} all-gather(bf16[1,1,768]{2,1,0:T(2,128)(2,1)S(1)} %reshape.59), channel_id=5, replica_groups=mesh['expert'=32,'hid'=1] {'expert'}, dimensions={0}, use_global_device_ids=true | all-gather | bytes 50688 | tf_op jit(solution)/shard_map/all_gather | solution.py:146
  382.6 0.3 reduce.1
  382.8 0.4 reshape.53
  383.3 0.1 copy.32
  383.3 0.1 copy.41
  383.4 0.2 fusion.29
  383.6 0.6 select_reduce_fusion
  384.2 24.3 %reduce-scatter.2.cloned.1.call-done = bf16[1,128,3584]{2,1,0:T(8,128)(2,1)} async-done(((bf16[4,128,3584]{2,1,0:T(8,128)(2,1)}), bf16[1,128,3584]{2,1,0:T(8,128)(2,1)}) %reduce-scatter.2.cloned.1.call-update) | async-done | bytes 917520 | tf_op jit(solution)/shard_map/reduce_scatter | solution.py:143
  (8 shorter events, 0.1 us)
Async XLA Ops:
  7.2 77.3 %all-gather.10.cloned.1.call-start = ((), (), s32[]{:S(2)}) async-start(), calls=%async_computation.6 | async-start | bytes 4587520 | tf_op jit(solution)/shard_map/all_gather | solution.py:110
  7.9 148.8 %all-gather.8.cloned.1.call-start = ((), (), s32[]{:S(2)}) async-start(), calls=%async_computation.5 | async-start | bytes 4587520 | tf_op jit(solution)/shard_map/all_gather | solution.py:110
  91.0 72.4 %all-to-all-start.1 = ((bf16[8,96,3584]{2,1,0:T(8,128)(2,1)}), bf16[8,96,3584]{2,1,0:T(8,128)(2,1)}, u32[]{:S(2)}, u32[]{:S(2)}) async-start(bf16[8,96,3584]{2,1,0:T(8,128)(2,1)} %bitcast.66), calls=%async_computation.1 | async-start | bytes 11010048 | tf_op jit(solution)/shard_map/all_to_all | solution.py:113
  163.3 67.9 %all-to-all-start = ((bf16[8,96,3584]{2,1,0:T(8,128)(2,1)}), bf16[8,96,3584]{2,1,0:T(8,128)(2,1)}, u32[]{:S(2)}, u32[]{:S(2)}) async-start(bf16[8,96,3584]{2,1,0:T(8,128)(2,1)} %bitcast.65), calls=%async_computation | async-start | bytes 11010048 | tf_op jit(solution)/shard_map/all_to_all | solution.py:113
  231.2 11.8 %copy-start.1 = (f32[768,1024]{1,0:T(8,128)S(1)}, f32[768,1024]{1,0:T(8,128)}, u32[]{:S(2)}) copy-start(f32[768,1024]{1,0:T(8,128)} %fusion.4) | copy-start | bytes 9437188
  231.2 11.8 %copy-start.2 = (f32[768,1024]{1,0:T(8,128)S(1)}, f32[768,1024]{1,0:T(8,128)}, u32[]{:S(2)}) copy-start(f32[768,1024]{1,0:T(8,128)} %fusion.8) | copy-start | bytes 9437188
  268.1 67.9 %all-to-all-start.2 = ((bf16[8,96,3584]{2,1,0:T(8,128)(2,1)}), bf16[8,96,3584]{2,1,0:T(8,128)(2,1)}, u32[]{:S(2)}, u32[]{:S(2)}) async-start(bf16[8,96,3584]{2,1,0:T(8,128)(2,1)} %bitcast.67), calls=%async_computation.2 | async-start | bytes 11010048 | tf_op jit(solution)/shard_map/all_to_all | solution.py:113
  272.8 135.8 %reduce-scatter.2.cloned.1.call-start = ((), (), s32[]{:S(2)}) async-start(), calls=%async_computation.4 | async-start | bytes 4587520 | tf_op jit(solution)/shard_map/reduce_scatter | solution.py:143
  342.7 0.7 copy-start
Sparse Core Ops, SparseCore 0:
  9.6 74.8 all-gather.9
  86.1 70.6 all-gather.7
  342.8 65.7 reduce-scatter.1

commit v2 on v1

--- a/solution.py
+++ b/solution.py
@@ -1,10 +1,15 @@
+import functools
+
 import jax
 import jax.numpy as jnp
 from jax import lax
+from jax.experimental import pallas as pl
+from jax.experimental.pallas import tpu as pltpu
 from jax.sharding import PartitionSpec as P
 
 BF = jnp.bfloat16
 F32 = jnp.float32
+MESH = pl.DeviceIdType.MESH
 
 
 def place_rows(source, dest_slot, slot_count):
@@ -83,78 +88,405 @@
     return grad_part, score_part
 
 
-def slot_masks(ids, experts, capacity):
-    tok_rows = ids.shape[-2]
-    hit = ids[..., None] == experts
-    named = jnp.any(hit, axis=-2).astype(BF)
-    before = jnp.tril(jnp.ones((tok_rows, tok_rows), BF), -1)
-    rank = jnp.einsum("ut,...te->...eu", before, named, preferred_element_type=F32)
-    named = jnp.swapaxes(named, -1, -2) > 0
-    slots = jnp.arange(capacity, dtype=F32)
-    place = (rank[..., None, :] == slots[:, None]) & named[..., None, :]
-    return hit, place
+def fused_kernel(
+    layers, plane, rows, cap, width, hidden, top, cw,
+    pk_ref, tok_ref, dout_ref, wg_ref, wu_ref, wd_ref, tg_ref, gg_ref,
+    pk, ag, snd, rcv, zsnd, zrcv, gz, gzr, sc, scr, pmat, chi, clo,
+    acc_g, acc_u, acc_h, ggp, gup, wgs, wus, wds,
+    own_sem, ag_ss, ag_rs, snd_ss, rcv_rs, ret_ss, ret_rs, z_ss, z_rs, mis_ss, mis_rs, w_sem,
+):
+    me = lax.axis_index("expert")
+    z = me // plane
+    q = me % plane
+    per = width // cw
+    chunks = 2 * per
+    blk = layers * cap
+    slots = plane * blk
+    toks = layers * rows
+
+    def dev(zz, qq):
+        return {"expert": zz * plane + qq}
+
+    def remote(src, dst, ss, rs, who):
+        return pltpu.make_async_remote_copy(
+            src_ref=src, dst_ref=dst, send_sem=ss, recv_sem=rs, device_id=who, device_id_type=MESH
+        )
+
+    def own_copy(c):
+        src = tok_ref if c < per else dout_ref
+        return pltpu.make_async_copy(
+            src.at[:, pl.ds((c % per) * cw, cw)], ag.at[c, z], own_sem.at[c]
+        )
+
+    for c in range(chunks):
+        own_copy(c).start()
+
+    def w_copies(c, slot):
+        at = pl.ds(pl.multiple_of(c * cw, cw), cw)
+        return (
+            pltpu.make_async_copy(wg_ref.at[at, :], wgs.at[slot], w_sem.at[0, slot]),
+            pltpu.make_async_copy(wu_ref.at[at, :], wus.at[slot], w_sem.at[1, slot]),
+        )
+
+    def wd_copy(c, slot):
+        at = pl.ds(pl.multiple_of(c * cw, cw), cw)
+        return pltpu.make_async_copy(wd_ref.at[:, at], wds.at[slot], w_sem.at[2, slot])
+
+    for cp in w_copies(0, 0):
+        cp.start()
+    wd_copy(0, 0).start()
+
+    barrier = pltpu.get_barrier_semaphore()
+    for j in range(1, plane):
+        pl.semaphore_signal(barrier, inc=1, device_id=dev(z, (q + j) % plane), device_id_type=MESH)
+    for r in range(1, layers):
+        pl.semaphore_signal(barrier, inc=1, device_id=dev((z + r) % layers, q), device_id_type=MESH)
+    pl.semaphore_wait(barrier, plane - 1 + layers - 1)
+
+    def z_all(src_of, dst, ss, rs):
+        for r in range(1, layers):
+            remote(src_of(r), dst.at[r], ss, rs, dev((z + r) % layers, q)).start()
+
+    def wait_both(buf, ss, rs):
+        done = remote(buf, buf, ss, rs, dev((z + 1) % layers, q))
+        done.wait_send()
+        done.wait_recv()
+
+    pk[0] = pk_ref[...]
+    z_all(lambda r: pk.at[0], pk, mis_ss.at[0], mis_rs.at[0])
+
+    def hop(c, h, way):
+        block = z - way * (h - 1)
+        d = 0 if way > 0 else 1
+        return remote(
+            ag.at[c, block], ag.at[c, block], ag_ss.at[c, h - 1, d], ag_rs.at[c, h - 1, d],
+            dev(z + way, q),
+        )
+
+    def sends(h, way):
+        edge = (z + 1 < layers) if way > 0 else (z >= 1)
+        has = (z - (h - 1) >= 0) if way > 0 else (z + (h - 1) < layers)
+        return jnp.logical_and(edge, has)
+
+    def gets(h, way):
+        return (z - h >= 0) if way > 0 else (z + h < layers)
+
+    def start_hop(c, h):
+        for way in (1, -1):
+            @pl.when(sends(h, way))
+            def _():
+                hop(c, h, way).start()
+
+    def wait_hop(c, h):
+        for way in (1, -1):
+            @pl.when(gets(h, way))
+            def _():
+                block = z - way * h
+                d = 0 if way > 0 else 1
+                remote(
+                    ag.at[c, block], ag.at[c, block], ag_ss.at[c, h - 1, d], ag_rs.at[c, h - 1, d],
+                    dev(z - way, q),
+                ).wait_recv()
+
+    def plane_send(src, dst, ss, rs, sign):
+        for j in range(1, plane):
+            remote(src.at[j], dst.at[j], ss, rs, dev(z, (q + sign * j + plane) % plane)).start()
+
+    def group(buf):
+        return buf.at[pl.ds(1, plane - 1)]
+
+    def masks():
+        wait_both(pk.at[pl.ds(1, layers - 1)], mis_ss.at[0], mis_rs.at[0])
+        jj = lax.broadcasted_iota(jnp.int32, (plane, rows), 0)
+        expert = (z * plane + (q + jj) % plane).astype(F32)
+        lower = lax.broadcasted_iota(jnp.int32, (rows, rows), 0) < lax.broadcasted_iota(
+            jnp.int32, (rows, rows), 1
+        )
+        upper = jnp.where(lower, 1.0, 0.0).astype(BF)
+        shape = (plane, layers, cap, rows)
+        row_z = lax.broadcasted_iota(jnp.int32, shape, 1)
+        row_s = lax.broadcasted_iota(jnp.int32, shape, 2).astype(F32)
+        for zs in range(layers):
+            info = pk[(z - zs + layers) % layers]
+            named = jnp.zeros((plane, rows), F32)
+            gate = jnp.zeros((plane, rows), F32)
+            for k in range(top):
+                same = info[k : k + 1, :] == expert
+                named = named + jnp.where(same, 1.0, 0.0)
+                gate = gate + jnp.where(same, info[top + k : top + k + 1, :], 0.0)
+            rank = jnp.dot(named.astype(BF), upper, preferred_element_type=F32)
+            rank = jnp.where(named > 0.5, rank, -1.0)
+            full = (row_s == rank[:, None, None, :]) & (row_z == zs)
+            one = jnp.where(full, 1.0, 0.0).reshape(slots, rows)
+            pmat[:, zs * rows : (zs + 1) * rows] = one.astype(BF)
+            wt = jnp.where(full, gate[:, None, None, :], 0.0).reshape(slots, rows).T
+            hi = wt.astype(BF)
+            chi[zs * rows : (zs + 1) * rows, :] = hi
+            clo[zs * rows : (zs + 1) * rows, :] = (wt - hi.astype(F32)).astype(BF)
+
+    masks()
+    for c in range(chunks):
+        own_copy(c).wait()
+    acc_g[...] = jnp.zeros_like(acc_g)
+    acc_u[...] = jnp.zeros_like(acc_u)
+    acc_h[...] = jnp.zeros_like(acc_h)
+    last = (((1,), (1,)), ((), ()))
+    tile = 256
+
+    def step(i, _):
+        @pl.when(i < chunks)
+        def _():
+            start_hop(i, 1)
+
+        for h in range(1, layers):
+            c = i - h
+
+            @pl.when(jnp.logical_and(c >= 0, c < chunks))
+            def _():
+                wait_hop(c, h)
+                if h < layers - 1:
+                    start_hop(c, h + 1)
+
+        c = i - (layers - 1)
+
+        @pl.when(jnp.logical_and(c >= 0, c < chunks))
+        def _():
+            slot = c % per
+
+            @pl.when(c >= per)
+            def _():
+                remote(
+                    group(snd.at[slot]), group(snd.at[slot]), snd_ss.at[c - per],
+                    rcv_rs.at[c - per], dev(z, (q + 1) % plane),
+                ).wait_send()
+
+            built = jnp.dot(pmat[...], ag[c].reshape(toks, cw), preferred_element_type=F32)
+            built = built.astype(BF).reshape(plane, blk, cw)
+            snd[slot] = built
+            rcv[c, 0] = built[0]
+            plane_send(snd.at[slot], rcv.at[c], snd_ss.at[c], rcv_rs.at[c], 1)
+
+        c2 = i - (layers + 1)
+
+        @pl.when(c2 >= 0)
+        def _():
+            remote(
+                group(rcv.at[c2]), group(rcv.at[c2]), snd_ss.at[c2], rcv_rs.at[c2],
+                dev(z, (q + 1) % plane),
+            ).wait_recv()
+            ws = c2 % 2
+
+            @pl.when(c2 < per)
+            def _():
+                for cp in w_copies(c2, ws):
+                    cp.wait()
+
+                @pl.when(c2 + 1 < per)
+                def _():
+                    for cp in w_copies(c2 + 1, (c2 + 1) % 2):
+                        cp.start()
+
+                @pl.loop(0, hidden // tile)
+                def _(t):
+                    at = pl.ds(pl.multiple_of(t * tile, tile), tile)
+                    xr = rcv[c2].reshape(slots, cw)
+                    acc_g[:, at] += jnp.dot(xr, wgs[ws, :, at], preferred_element_type=F32)
+                    acc_u[:, at] += jnp.dot(xr, wus[ws, :, at], preferred_element_type=F32)
+
+            @pl.when(c2 >= per)
+            def _():
+                c3 = c2 - per
+                wd_copy(c3, c3 % 2).wait()
+
+                @pl.when(c3 + 1 < per)
+                def _():
+                    wd_copy(c3 + 1, (c3 + 1) % 2).start()
+
+                @pl.when(c3 == 0)
+                def _():
+                    for cp in w_copies(0, 0):
+                        cp.start()
+
+                @pl.loop(0, hidden // tile)
+                def _(t):
+                    at = pl.ds(pl.multiple_of(t * tile, tile), tile)
+                    dr = rcv[c2].reshape(slots, cw)
+                    acc_h[:, at] += lax.dot_general(
+                        dr, wds[c3 % 2, at, :], last, preferred_element_type=F32
+                    )
+
+        return 0
+
+    lax.fori_loop(0, chunks + layers + 1, step, 0)
+
+    for j in range(plane):
+        at = pl.ds(j * blk, blk)
+        g, u, d = acc_g[at, :], acc_u[at, :], acc_h[at, :]
+        sig = jax.nn.sigmoid(g)
+        act = g * sig
+        score = jnp.sum(act * u * d, axis=1, keepdims=True)
+        sc[j] = jnp.broadcast_to(score, (blk, rows)).astype(BF)
+        ggp[at, :] = (d * u * sig * (1.0 + g * (1.0 - sig))).astype(BF)
+        gup[at, :] = (d * act).astype(BF)
+
+    scr[0] = sc[0]
+    plane_send(sc, scr, mis_ss.at[1], mis_rs.at[1], -1)
+
+    def back(i, _):
+        @pl.when(i < per)
+        def _():
+            ws = i % 2
+            for cp in w_copies(i, ws):
+                cp.wait()
+
+            @pl.when(i + 1 < per)
+            def _():
+                for cp in w_copies(i + 1, (i + 1) % 2):
+                    cp.start()
+
+            remote(
+                group(snd.at[i]), group(snd.at[i]), snd_ss.at[per + i], rcv_rs.at[per + i],
+                dev(z, (q + 1) % plane),
+            ).wait_send()
+            grad = lax.dot_general(ggp[...], wgs[ws], last, preferred_element_type=F32)
+            grad = grad + lax.dot_general(gup[...], wus[ws], last, preferred_element_type=F32)
+            out = grad.astype(BF).reshape(plane, blk, cw)
+            snd[i] = out
+            rcv[i, 0] = out[0]
+            plane_send(snd.at[i], rcv.at[i], ret_ss.at[i], ret_rs.at[i], -1)
+
+        c = i - 2
+
+        @pl.when(c >= 0)
+        def _():
+            done = remote(
+                group(rcv.at[c]), group(rcv.at[c]), ret_ss.at[c], ret_rs.at[c],
+                dev(z, (q + 1) % plane),
+            )
+            done.wait_send()
+            done.wait_recv()
+            rr = rcv[c].reshape(slots, cw)
+            part = jnp.dot(chi[...], rr, preferred_element_type=F32)
+            part = part + jnp.dot(clo[...], rr, preferred_element_type=F32)
+            zsnd[c] = part.astype(BF).reshape(layers, rows, cw)
+            z_all(lambda r: zsnd.at[c, (z + r) % layers], zrcv.at[c], z_ss.at[c], z_rs.at[c])
+
+        return 0
+
+    lax.fori_loop(0, per + 2, back, 0)
+
+    wait_both(group(scr), mis_ss.at[1], mis_rs.at[1])
+    jj = lax.broadcasted_iota(jnp.int32, (plane, rows), 0)
+    expert = (z * plane + (q + jj) % plane).astype(F32)
+    val = scr[...].astype(F32).reshape(slots, rows)
+    for zs in range(layers):
+        info = pk[(z - zs + layers) % layers]
+        hold = pmat[:, zs * rows : (zs + 1) * rows].astype(F32) * val
+        by = jnp.sum(hold.reshape(plane, blk, rows), axis=1)
+        parts = [
+            jnp.sum(jnp.where(info[k : k + 1, :] == expert, by, 0.0), axis=0, keepdims=True)
+            for k in range(top)
+        ]
+        gz[zs] = jnp.concatenate(parts + [jnp.zeros((8 - top, rows), F32)], axis=0)
+    z_all(lambda r: gz.at[(z + r) % layers], gzr, mis_ss.at[2], mis_rs.at[2])
+
+    for c in range(per):
+        wait_both(zrcv.at[c, pl.ds(1, layers - 1)], z_ss.at[c], z_rs.at[c])
+        total = zsnd[c, z].astype(F32)
+        for r in range(1, layers):
+            total = total + zrcv[c, r].astype(F32)
+        tg_ref[:, c * cw : (c + 1) * cw] = total.astype(BF)
+
+    wait_both(gzr.at[pl.ds(1, layers - 1)], mis_ss.at[2], mis_rs.at[2])
+    total = gz[z]
+    for r in range(1, layers):
+        total = total + gzr[r]
+    gg_ref[...] = total
+
+    def drain(c, _):
+        for h in range(1, layers):
+            for way in (1, -1):
+                @pl.when(sends(h, way))
+                def _():
+                    hop(c, h, way).wait_send()
+        return 0
+
+    lax.fori_loop(0, chunks, drain, 0)
 
 
 def plane_body(tokens, out_grad, route_ids, route_gates, w_gate, w_up, w_down):
     n = lax.axis_size("expert")
     plane = 8
     layers = n // plane
-    tok_rows, width = tokens.shape
-    top_count = route_ids.shape[1]
-    capacity = 3 * tok_rows * top_count // (2 * n)
-    me = lax.axis_index("expert")
-    columns = [[z * plane + q for z in range(layers)] for q in range(plane)]
-    planes = [[z * plane + q for q in range(plane)] for z in range(layers)]
-
-    def gather_z(a):
-        return lax.all_gather(a, "expert", axis_index_groups=columns)
-
-    def swap(a):
-        return lax.all_to_all(
-            a, "expert", split_axis=0, concat_axis=0, axis_index_groups=planes, tiled=True
-        )
-
-    packed = jnp.concatenate([route_ids.astype(F32), route_gates], axis=1)
-    packed = gather_z(packed)
-    all_x = gather_z(tokens)
-    all_d = gather_z(out_grad)
-    ids = packed[..., :top_count].astype(jnp.int32)
-    gates = packed[..., top_count:]
-    local = (me // plane) * plane + jnp.arange(plane, dtype=jnp.int32)
-    hit, place = slot_masks(ids, local, capacity)
-    gate_of = jnp.einsum("ztke,ztk->zet", hit.astype(F32), gates, precision="highest")
-    place_bf = place.astype(BF)
-    weights = jnp.where(place, gate_of[:, :, None, :], 0.0)
-    high = weights.astype(BF)
-    low = (weights - high.astype(F32)).astype(BF)
-
-    def dispatch(rows):
-        send = jnp.einsum("zest,ztd->ezsd", place_bf, rows, preferred_element_type=F32).astype(BF)
-        return swap(send.reshape(plane, layers * capacity, width)).reshape(-1, width)
-
-    rows_x = dispatch(all_x)
-    rows_d = dispatch(all_d)
-    grad_part, score = expert_math(rows_x, rows_d, w_gate[0], w_up[0], w_down[0])
-    back = swap(grad_part.astype(BF).reshape(plane, layers * capacity, width))
-    back = back.reshape(plane, layers, capacity, width)
-    both = jnp.concatenate([high, low], axis=1)
-    back2 = jnp.concatenate([back, back], axis=0)
-    part = jnp.einsum("zest,ezsd->ztd", both, back2, preferred_element_type=F32)
-    token_grad = lax.psum_scatter(
-        part.astype(BF), "expert", scatter_dimension=0, axis_index_groups=columns, tiled=False
-    )
-    scores = lax.all_gather(score.astype(BF), "expert").reshape(n, plane, layers, capacity)
-    mine = lax.dynamic_index_in_dim(scores, me % plane, 1, keepdims=False)
-    mine = lax.dynamic_index_in_dim(mine, me // plane, 1, keepdims=False)
-    hit_own, place_own = slot_masks(route_ids, jnp.arange(n, dtype=jnp.int32), capacity)
-    by_expert = jnp.einsum("est,es->te", place_own.astype(F32), mine.astype(F32), precision="highest")
-    gate_grad = jnp.sum(jnp.where(hit_own, by_expert[:, None, :], 0.0), axis=2).astype(BF)
-    return (token_grad, gate_grad)
+    rows, width = tokens.shape
+    hidden = w_gate.shape[2]
+    top = route_ids.shape[1]
+    cap = 3 * rows * top // (2 * n)
+    cw = 512
+    per = width // cw
+    blk = layers * cap
+    slots = plane * blk
+    toks = layers * rows
+    packed = jnp.concatenate([route_ids.astype(F32), route_gates], axis=1).T
+    vm = pl.BlockSpec(memory_space=pltpu.VMEM)
+    hbm = pl.BlockSpec(memory_space=pl.ANY)
+    dma = pltpu.SemaphoreType.DMA
+    token_grad, gates_t = pl.pallas_call(
+        functools.partial(fused_kernel, layers, plane, rows, cap, width, hidden, top, cw),
+        out_shape=(
+            jax.ShapeDtypeStruct((rows, width), BF),
+            jax.ShapeDtypeStruct((8, rows), F32),
+        ),
+        in_specs=[vm, hbm, hbm, hbm, hbm, hbm],
+        out_specs=(vm, vm),
+        scratch_shapes=[
+            pltpu.VMEM((layers, 8, rows), F32),
+            pltpu.VMEM((2 * per, layers, rows, cw), BF),
+            pltpu.VMEM((per, plane, blk, cw), BF),
+            pltpu.VMEM((2 * per, plane, blk, cw), BF),
+            pltpu.VMEM((per, layers, rows, cw), BF),
+            pltpu.VMEM((per, layers, rows, cw), BF),
+            pltpu.VMEM((layers, 8, rows), F32),
+            pltpu.VMEM((layers, 8, rows), F32),
+            pltpu.VMEM((plane, blk, rows), BF),
+            pltpu.VMEM((plane, blk, rows), BF),
+            pltpu.VMEM((slots, toks), BF),
+            pltpu.VMEM((toks, slots), BF),
+            pltpu.VMEM((toks, slots), BF),
+            pltpu.VMEM((slots, hidden), F32),
+            pltpu.VMEM((slots, hidden), F32),
+            pltpu.VMEM((slots, hidden), F32),
+            pltpu.VMEM((slots, hidden), BF),
+            pltpu.VMEM((slots, hidden), BF),
+            pltpu.VMEM((2, cw, hidden), BF),
+            pltpu.VMEM((2, cw, hidden), BF),
+            pltpu.VMEM((2, hidden, cw), BF),
+            dma((2 * per,)),
+            dma((2 * per, layers - 1, 2)),
+            dma((2 * per, layers - 1, 2)),
+            dma((2 * per,)),
+            dma((2 * per,)),
+            dma((per,)),
+            dma((per,)),
+            dma((per,)),
+            dma((per,)),
+            dma((3,)),
+            dma((3,)),
+            dma((3, 2)),
+        ],
+        compiler_params=pltpu.CompilerParams(
+            collective_id=0, has_side_effects=True, vmem_limit_bytes=64 * 1024 * 1024 - 65536
+        ),
+        cost_estimate=pl.CostEstimate(
+            flops=10 * slots * width * hidden, bytes_accessed=10 * width * hidden, transcendentals=0
+        ),
+    )(packed, tokens, out_grad, w_gate[0], w_up[0], w_down[0])
+    return (token_grad, gates_t[:top].T.astype(BF))
 
 
 def solution(mesh):
     n = mesh.shape["expert"]
-    flat = mesh.shape["hid"] != 1 or n % 8 != 0
+    flat = mesh.shape["hid"] != 1 or n != 32
     return jax.shard_map(
         flat_body if flat else plane_body,
         mesh=mesh,

time: 416 us -> 253 us (0.61)
  waiting for transfers between devices: 250 us -> 0 us
  Pallas kernels: 0 us -> 246 us
  matrix products: 73.2 us -> 0 us
  blocking collectives: 53.9 us -> 0 us
  starting transfers between devices: 14.3 us -> 0 us
  between operations: 13.9 us -> 0.64 us
  local copies, waits for them, and re-layouts: 7.04 us -> 2.72 us
    pallas_call x0 -> x1, Pallas kernels: none -> 246 us  [plane_body(): pl.pallas_call(functools.partial(fused_kernel, layers, plane, rows, cap,...]
    all_gather x2 -> x0, waiting for transfers between devices: 120 us -> none  [gather_z(): return lax.all_gather(a, 'expert', axis_index_groups=columns)]
    all_to_all x3 -> x0, waiting for transfers between devices: 104 us -> none  [swap(): lax.all_to_all(a, 'expert', split_axis=0, concat_axis=0, axis_index_group...]
    dot_general x11 -> x0, matrix products: 73.2 us -> none  [the longest x1 12.7 us: expert_math(): lax.dot_general(grad_gate_pre, gate_mat, contract_last, preferred_element...]
    all_gather x2 -> x0, blocking collectives: 53.9 us -> none  [the longest x1 39 us: plane_body(): lax.all_gather(score.astype(BF), 'expert')]
    reduce_scatter x1 -> x0, waiting for transfers between devices: 24.3 us -> none  [plane_body(): lax.psum_scatter(part.astype(BF), 'expert', scatter_dimension=0, axis_ind...]
    all_to_all x3 -> x0, starting transfers between devices: 14.2 us -> none  [swap(): lax.all_to_all(a, 'expert', split_axis=0, concat_axis=0, axis_index_group...]
    convert_element_type x2 -> x1, local copies, waits for them, and re-layouts: 5.81 us -> 0.57 us  [plane_body(): return (token_grad, gates_t[:top].T.astype(BF))]
  transfers between devices with their start and end apart: 6 -> 0, of which waited for: 5 -> 0; matrix products, arithmetic and copies ran while one was open for 9% -> 0% of each run, Pallas kernels for 0% -> 0%
where the time goes in v2:
time: 253 us; the launch traced here: 252 us
  Pallas kernels  246 us (97%)
  local copies, waits for them, and re-layouts  2.72 us (1%)
  other arithmetic  2.64 us (1%)
    pallas_call x1, Pallas kernels, plane_body(): pl.pallas_call(functools.partial(fused_kernel, layers, plane, rows, cap,...  246 us

profile of v2, /device:TPU:0, one launch (start us, length us, event | category | flops | bytes accessed | tf_op | source)
XLA Modules:
  0.0 252.3 jit_solution(1409696697817637350)
XLA Ops:
  0.6 0.7 convert_element_type.7
  1.3 1.3 maximum_bitcast_fusion.pk_ref
  2.6 246.2 %shard_map.86 = (bf16[128,3584]{1,0:T(8,128)(2,1)}, f32[8,128]{1,0:T(8,128)}) custom-call(f32[8,128]{1,0:T(8,128)} %maximum_bitcast_fusion.pk_ref, bf16[128,3584]{1,0:T(8,128)(2,1)} %tok_ref.1, bf16[128,3584]{1,0:T(8,128)(2,1)} %dout_ref.1, bf16[3584,1024]{1,0:T(8,128)(2,1)} %bitcast.7, bf16[3584,1024]{1,0:T(8,128)(2,1)} %bitcast.8, bf16[1024,3584]{1,0:T(8,128)(2,1)} %bitcast.9), custom_call_target="tpu_custom_call" | custom-call | flops 28185722880 | bytes 36700160 | tf_op jit(solution)/shard_map/pallas_call | solution.py:434
  248.9 0.7 convert.3
  249.5 0.6 slice_bitcast_fusion
  250.1 2.2 copy.10

commit v3 on v2

--- a/solution.py
+++ b/solution.py
@@ -224,9 +224,11 @@
             chi[zs * rows : (zs + 1) * rows, :] = hi
             clo[zs * rows : (zs + 1) * rows, :] = (wt - hi.astype(F32)).astype(BF)
 
-    masks()
     for c in range(chunks):
         own_copy(c).wait()
+    start_hop(0, 1)
+    start_hop(1, 1)
+    masks()
     acc_g[...] = jnp.zeros_like(acc_g)
     acc_u[...] = jnp.zeros_like(acc_u)
     acc_h[...] = jnp.zeros_like(acc_h)
@@ -234,7 +236,7 @@
     tile = 256
 
     def step(i, _):
-        @pl.when(i < chunks)
+        @pl.when(jnp.logical_and(i >= 2, i < chunks))
         def _():
             start_hop(i, 1)
 
@@ -331,6 +333,35 @@
 
     scr[0] = sc[0]
     plane_send(sc, scr, mis_ss.at[1], mis_rs.at[1], -1)
+
+    outer = jnp.logical_or(z == 0, z == layers - 1)
+    inner = jnp.logical_not(outer)
+    beside = z + 1 - 2 * (z % 2)
+    across, far = layers - 1 - z, layers - 1 - beside
+
+    def to_layer(c, block, slot, who, turn):
+        return remote(
+            zsnd.at[c, block], zrcv.at[c, slot], z_ss.at[c, turn], z_rs.at[c, turn], dev(who, q)
+        )
+
+    def landed(c, start, count, turn):
+        some = zrcv.at[c, pl.ds(start, count)]
+        return remote(some, some, z_ss.at[c, turn], z_rs.at[c, turn], dev(beside, q))
+
+    def first_hop(c):
+        to_layer(c, beside, 0, beside, 0).start()
+
+        @pl.when(outer)
+        def _():
+            to_layer(c, far, 1, beside, 0).start()
+            to_layer(c, across, 2, beside, 0).start()
+
+    def second_hop(c):
+        landed(c, 0, 3, 0).wait_recv()
+        for block, slot in ((across, 1), (far, 2)):
+            both = zsnd[c, block].astype(F32) + zrcv[c, slot].astype(F32)
+            zsnd[c, block] = both.astype(BF)
+            to_layer(c, block, 3, block, 1).start()
 
     def back(i, _):
         @pl.when(i < per)
@@ -357,7 +388,7 @@
 
         c = i - 2
 
-        @pl.when(c >= 0)
+        @pl.when(jnp.logical_and(c >= 0, c < per))
         def _():
             done = remote(
                 group(rcv.at[c]), group(rcv.at[c]), ret_ss.at[c], ret_rs.at[c],
@@ -369,11 +400,17 @@
             part = jnp.dot(chi[...], rr, preferred_element_type=F32)
             part = part + jnp.dot(clo[...], rr, preferred_element_type=F32)
             zsnd[c] = part.astype(BF).reshape(layers, rows, cw)
-            z_all(lambda r: zsnd.at[c, (z + r) % layers], zrcv.at[c], z_ss.at[c], z_rs.at[c])
+            first_hop(c)
+
+        b = i - 3
+
+        @pl.when(jnp.logical_and(b >= 0, inner))
+        def _():
+            second_hop(b)
 
         return 0
 
-    lax.fori_loop(0, per + 2, back, 0)
+    lax.fori_loop(0, per + 3, back, 0)
 
     wait_both(group(scr), mis_ss.at[1], mis_rs.at[1])
     jj = lax.broadcasted_iota(jnp.int32, (plane, rows), 0)
@@ -391,10 +428,18 @@
     z_all(lambda r: gz.at[(z + r) % layers], gzr, mis_ss.at[2], mis_rs.at[2])
 
     for c in range(per):
-        wait_both(zrcv.at[c, pl.ds(1, layers - 1)], z_ss.at[c], z_rs.at[c])
-        total = zsnd[c, z].astype(F32)
-        for r in range(1, layers):
-            total = total + zrcv[c, r].astype(F32)
+        @pl.when(outer)
+        def _():
+            landed(c, 0, 1, 0).wait_recv()
+            landed(c, 0, 3, 0).wait_send()
+
+        @pl.when(inner)
+        def _():
+            landed(c, 0, 1, 0).wait_send()
+            landed(c, 0, 2, 1).wait_send()
+
+        landed(c, 3, 1, 1).wait_recv()
+        total = zsnd[c, z].astype(F32) + zrcv[c, 0].astype(F32) + zrcv[c, 3].astype(F32)
         tg_ref[:, c * cw : (c + 1) * cw] = total.astype(BF)
 
     wait_both(gzr.at[pl.ds(1, layers - 1)], mis_ss.at[2], mis_rs.at[2])
@@ -468,8 +513,8 @@
             dma((2 * per,)),
             dma((per,)),
             dma((per,)),
-            dma((per,)),
-            dma((per,)),
+            dma((per, 2)),
+            dma((per, 2)),
             dma((3,)),
             dma((3,)),
             dma((3, 2)),

time: 253 us -> 238 us (0.941)
  Pallas kernels: 246 us -> 231 us
    pallas_call x1, Pallas kernels: 246 us -> 231 us  [plane_body(): pl.pallas_call(functools.partial(fused_kernel, layers, plane, rows, cap,...]
where the time goes in v3:
time: 238 us; the launch traced here: 237 us
  Pallas kernels  231 us (97%)
  local copies, waits for them, and re-layouts  2.72 us (1%)
  other arithmetic  2.64 us (1%)
    pallas_call x1, Pallas kernels, plane_body(): pl.pallas_call(functools.partial(fused_kernel, layers, plane, rows, cap,...  231 us

profile of v3, /device:TPU:0, one launch (start us, length us, event | category | flops | bytes accessed | tf_op | source)
XLA Modules:
  0.0 237.3 jit_solution(14782710861095270600)
XLA Ops:
  0.6 0.7 convert_element_type.7
  1.3 1.3 maximum_bitcast_fusion.pk_ref
  2.6 231.3 %shard_map.86 = (bf16[128,3584]{1,0:T(8,128)(2,1)}, f32[8,128]{1,0:T(8,128)}) custom-call(f32[8,128]{1,0:T(8,128)} %maximum_bitcast_fusion.pk_ref, bf16[128,3584]{1,0:T(8,128)(2,1)} %tok_ref.1, bf16[128,3584]{1,0:T(8,128)(2,1)} %dout_ref.1, bf16[3584,1024]{1,0:T(8,128)(2,1)} %bitcast.7, bf16[3584,1024]{1,0:T(8,128)(2,1)} %bitcast.8, bf16[1024,3584]{1,0:T(8,128)(2,1)} %bitcast.9), custom_call_target="tpu_custom_call" | custom-call | flops 28185722880 | bytes 36700160 | tf_op jit(solution)/shard_map/pallas_call | solution.py:479
  233.9 0.7 convert.3
  234.6 0.6 slice_bitcast_fusion
  235.2 2.2 copy.10

commit v4 on v3

--- a/solution.py
+++ b/solution.py
@@ -321,7 +321,15 @@
 
     lax.fori_loop(0, chunks + layers + 1, step, 0)
 
-    for j in range(plane):
+    for cp in w_copies(0, 0):
+        cp.wait()
+    for cp in w_copies(1, 1):
+        cp.start()
+    remote(
+        group(snd.at[0]), group(snd.at[0]), snd_ss.at[per], rcv_rs.at[per],
+        dev(z, (q + 1) % plane),
+    ).wait_send()
+    for j in list(range(1, plane)) + [0]:
         at = pl.ds(j * blk, blk)
         g, u, d = acc_g[at, :], acc_u[at, :], acc_h[at, :]
         sig = jax.nn.sigmoid(g)
@@ -330,6 +338,16 @@
         sc[j] = jnp.broadcast_to(score, (blk, rows)).astype(BF)
         ggp[at, :] = (d * u * sig * (1.0 + g * (1.0 - sig))).astype(BF)
         gup[at, :] = (d * act).astype(BF)
+        grad = lax.dot_general(ggp[at, :], wgs[0], last, preferred_element_type=F32)
+        grad = grad + lax.dot_general(gup[at, :], wus[0], last, preferred_element_type=F32)
+        snd[0, j] = grad.astype(BF)
+        if j == 0:
+            rcv[0, 0] = grad.astype(BF)
+        else:
+            remote(
+                snd.at[0, j], rcv.at[0, j], ret_ss.at[0], ret_rs.at[0],
+                dev(z, (q - j + plane) % plane),
+            ).start()
 
     scr[0] = sc[0]
     plane_send(sc, scr, mis_ss.at[1], mis_rs.at[1], -1)
@@ -410,7 +428,7 @@
 
         return 0
 
-    lax.fori_loop(0, per + 3, back, 0)
+    lax.fori_loop(1, per + 3, back, 0)
 
     wait_both(group(scr), mis_ss.at[1], mis_rs.at[1])
     jj = lax.broadcasted_iota(jnp.int32, (plane, rows), 0)

time: 238 us -> 239 us (level)
  no operation moved by 1% of the time
where the time goes in v4:
time: 239 us; the launch traced here: 238 us
  Pallas kernels  232 us (97%)
  local copies, waits for them, and re-layouts  2.72 us (1%)
  other arithmetic  2.64 us (1%)
    pallas_call x1, Pallas kernels, plane_body(): pl.pallas_call(functools.partial(fused_kernel, layers, plane, rows, cap,...  232 us

profile of v4, /device:TPU:0, one launch (start us, length us, event | category | flops | bytes accessed | tf_op | source)
XLA Modules:
  0.0 238.3 jit_solution(2389032322316632031)
XLA Ops:
  0.6 0.7 convert_element_type.7
  1.3 1.3 maximum_bitcast_fusion.pk_ref
  2.6 232.3 %shard_map.86 = (bf16[128,3584]{1,0:T(8,128)(2,1)}, f32[8,128]{1,0:T(8,128)}) custom-call(f32[8,128]{1,0:T(8,128)} %maximum_bitcast_fusion.pk_ref, bf16[128,3584]{1,0:T(8,128)(2,1)} %tok_ref.1, bf16[128,3584]{1,0:T(8,128)(2,1)} %dout_ref.1, bf16[3584,1024]{1,0:T(8,128)(2,1)} %bitcast.7, bf16[3584,1024]{1,0:T(8,128)(2,1)} %bitcast.8, bf16[1024,3584]{1,0:T(8,128)(2,1)} %bitcast.9), custom_call_target="tpu_custom_call" | custom-call | flops 28185722880 | bytes 36700160 | tf_op jit(solution)/shard_map/pallas_call | solution.py:497
  234.9 0.7 convert.3
  235.6 0.6 slice_bitcast_fusion
  236.1 2.2 copy.10
